TPU v7x, 256 devices: a whole 4x4x8 slice. The times are simulated.
256 devices in a mesh: section: 2 (over x_hi), dp: 32 (over z, x_lo, core), tensor: 4 (over y).
Axes of the slice: x: 4 (x_hi: 2, x_lo: 2; x = x_hi * 2 + x_lo), y: 4, z: 8, core: 2. Of those that a mesh axis runs over, the one named last changes fastest.
Arguments:
- left: bfloat16 [2, 16384, 8192], P('section', 'dp', 'tensor'), may hold values from -6 to 6
- weight: bfloat16 [2, 8192, 5120], P('section', ('tensor', 'dp')), may hold values from -0.0625 to 0.0625
- base: bfloat16 [2, 16384, 5120], P('section', 'dp', 'tensor'), may hold values from -6 to 6
- expo: int32 [2, 128, 40], P('section', 'dp', 'tensor'), may hold values from -7 to 2
- perm: int32 [2, 32, 4], P('section', 'dp'), may hold values from 0 to 3, each once within a row
Outputs:
- received: float32 [2, 16384, 5120], P('section', ('dp', 'tensor'))
Inputs may be any that keep to these rules, and one draw needn't show every extreme that they name: Each row of perm holds every number from 0 to 3 once.
All inputs are finite; a program needn't handle non-finite values.
Results may differ from a plain program's by a relative error of at most 0.01.
Values may be sent and summed in bfloat16 or wider, within the bound.
No kernel may reach another device: no remote copies, remote signals or barrier semaphores. Data moves between devices by JAX's collectives and lax.ppermute only.
A program may use at most 128 MiB of HBM per device.

v0:
```python
import math

import jax
import jax.numpy as jnp
from jax import lax
from jax.sharding import PartitionSpec as P

TILE = 128


def as_sent(array):

    def short(part):
        return part.astype(jnp.bfloat16) if part.dtype == jnp.float32 else part

    return jax.tree.map(short, array)


def from_behind(value, axis, steps):
    count = lax.axis_size(axis)
    pairs = [(source, (source + steps) % count) for source in range(count)]
    return lax.ppermute(value, axis, pairs)


def hadamard(size):
    index = jnp.arange(size, dtype=jnp.int32)
    common = jnp.bitwise_and(index[:, None], index[None, :])
    parity = jnp.zeros((size, size), jnp.int32)
    for shift_bit in range(size.bit_length() - 1):
        parity = parity + jnp.bitwise_and(jnp.right_shift(common, shift_bit), 1)
    signs = 1 - 2 * jnp.bitwise_and(parity, 1)
    return signs.astype(jnp.float32) / math.sqrt(size)


def rotate(values, table):
    size = table.shape[0]
    rows, cols = values.shape
    tiles = values.reshape(rows // size, size, cols // size, size)
    turned = jnp.einsum("aibj,jk->aibk", tiles, table, precision=lax.Precision.HIGHEST)
    return turned.reshape(rows, cols)


def quantize(values, exponent, table):
    size = table.shape[0]
    rows, cols = values.shape
    turned = rotate(values, table).reshape(rows // size, size, cols // size, size)
    scaled = turned * jnp.exp2(-exponent.astype(jnp.float32))[:, None, :, None]
    return jnp.clip(scaled.astype(jnp.bfloat16), -448.0, 448.0).reshape(rows, cols)


def restore(quant, exponent, table):
    size = table.shape[0]
    rows, cols = quant.shape
    values = quant.astype(jnp.float32).reshape(rows // size, size, cols // size, size)
    values = values * jnp.exp2(exponent.astype(jnp.float32))[:, None, :, None]
    return rotate(values.reshape(rows, cols), table)


def order_blocks(values, dest, count):
    positions = jnp.arange(count, dtype=jnp.int32)
    inverse = jnp.sum(jnp.where(dest[:, None] == positions[None, :], positions[:, None], 0), axis=0)
    shaped = values.reshape(count, values.shape[0] // count, values.shape[1])
    return jnp.take(shaped, inverse, axis=0).reshape(values.shape)


def cross(quant, exponent):
    return (
        from_behind(quant, "section", 1),
        from_behind(as_sent(exponent), "section", 1).astype(exponent.dtype),
    )


def relayout(quant, exponent):
    return (
        lax.all_to_all(quant, "tensor", split_axis=0, concat_axis=1, tiled=True),
        lax.all_to_all(exponent, "tensor", split_axis=0, concat_axis=1, tiled=True),
    )


def shards(left, weight, base, expo, perm):
    table = hadamard(TILE)
    left_rows = left[0]
    rows = left_rows.shape[0]
    count = rows // TILE
    dest = perm[0, 0]
    partial_value = jnp.dot(
        left_rows,
        lax.all_gather(weight[0], "dp", axis=0, tiled=True),
        preferred_element_type=jnp.float32,
    )
    feat = base.shape[2]
    col_start = lax.axis_index("tensor") * feat
    own_cols = lax.dynamic_slice_in_dim(partial_value, col_start, feat, 1) + base[0].astype(
        jnp.float32
    )
    partial_value = lax.dynamic_update_slice_in_dim(partial_value, own_cols, col_start, 1)
    summed = lax.psum_scatter(
        partial_value.astype(jnp.bfloat16), "tensor", scatter_dimension=1, tiled=True
    ).astype(jnp.float32)
    quant = quantize(summed, expo[0], table)
    quant = order_blocks(quant, dest, count)
    expo_here = order_blocks(expo[0], dest, count)
    quant, expo_here = relayout(quant, expo_here)
    quant, expo_here = cross(quant, expo_here)
    return restore(quant, expo_here, table)[None]


def solution(mesh):
    in_specs = (
        P("section", "dp", "tensor"),
        P("section", ("tensor", "dp"), None),
        P("section", "dp", "tensor"),
        P("section", "dp", "tensor"),
        P("section", "dp", None),
    )
    out_specs = P("section", ("dp", "tensor"), None)
    return jax.shard_map(shards, mesh=mesh, in_specs=in_specs, out_specs=out_specs, check_vma=False)
```

profile of v0, /device:TPU:1, one launch (start us, length us, event | category | flops | bytes accessed | tf_op | source)
XLA Modules:
  0.0 285.2 jit_solution(2844785938271687073)
XLA Ops:
  6.5 0.7 all-gather.3.cloned.1.call-update
  7.3 0.0 reduce-scatter.2.cloned.1.call-start
  7.3 127.0 %all-gather.3.cloned.1.call-done = bf16[1,2048,5120]{2,1,0:T(8,128)(2,1)} async-done(((bf16[1,64,5120]{2,1,0:T(8,128)(2,1)}), bf16[1,2048,5120]{2,1,0:T(8,128)(2,1)}) %all-gather.3.cloned.1.call-update) | async-done | bytes 20971536 | tf_op jit(solution)/shard_map/all_gather | solution.py:88
  134.3 14.0 %fusion = f32[512,5120]{1,0:T(8,128)S(1)} fusion(bf16[1,2048,5120]{2,1,0:T(8,128)(2,1)} %all-gather.3.cloned.1.call-done, bf16[1,512,2048]{2,1,0:T(8,128)(2,1)S(1)} %copy-done), kind=kOutput, calls=%fused_computation.2 | convolution fusion | flops 10737418240 | bytes 33554432 | tf_op jit(solution)/shard_map/dot_general | solution.py:86
  148.4 0.5 fusion.3
  148.9 3.1 %convert_element_type.36 = bf16[512,5120]{1,0:T(8,128)(2,1)} convert(f32[512,5120]{1,0:T(8,128)S(1)} %fusion.3) | non-fusion elementwise | flops 2621440 | bytes 15728640 | tf_op jit(solution)/shard_map/convert_element_type | solution.py:98
  152.0 0.6 copy-done.3
  152.6 0.1 select_reduce_fusion
  152.8 57.4 %reduce-scatter.2.cloned.1.call-done = bf16[512,1280]{1,0:T(8,128)(2,1)} async-done(((bf16[512,5120]{1,0:T(8,128)(2,1)}), bf16[512,1280]{1,0:T(8,128)(2,1)}) %reduce-scatter.2.cloned.1.call-update) | async-done | bytes 1310736 | tf_op jit(solution)/shard_map/reduce_scatter | solution.py:97
  210.2 3.7 %reshape.126 = bf16[4,128,10,128]{3,2,1,0:T(8,128)(2,1)} reshape(bf16[512,1280]{1,0:T(8,128)(2,1)} %reduce-scatter.2.cloned.1.call-done) | data formatting | bytes 2621440 | tf_op jit(solution)/shard_map/reshape | solution.py:38
  213.9 4.0 %fusion.5 = bf16[4,128,10,128]{1,3,2,0:T(8,128)(2,1)} fusion(bf16[4,128,10,128]{3,2,1,0:T(8,128)(2,1)} %reshape.126, f32[4,10]{1,0:T(4,128)S(1)} %exponential_bitcast_fusion), kind=kOutput, calls=%fused_computation.10 | convolution fusion | flops 1009025024 | bytes 2621600 | tf_op jit(solution)/shard_map/aibj,jk->aibk/dot_general | solution.py:39
  217.8 2.1 gather_fusion
  220.0 0.2 broadcast_select_fusion
  220.2 19.4 %all_to_all.29 = bf16[4,128,1280]{1,2,0:T(8,128)(2,1)S(1)} all-to-all(bf16[4,128,1280]{1,2,0:T(8,128)(2,1)S(1)} %broadcast_select_fusion), channel_id=1, replica_groups=mesh['section'=2,'dp'=32,'tensor'=4] {'tensor'}, dimensions={0} | all-to-all | bytes 2621440 | tf_op jit(solution)/shard_map/all_to_all | solution.py:75
  239.6 2.7 collective-permute-start
  242.3 0.6 gather_fusion.1
  242.8 0.1 bitcast_select_fusion
  242.9 6.8 %all_to_all.30 = s32[4,1,10]{2,1,0:T(1,128)S(1)} all-to-all(s32[4,1,10]{2,1,0:T(1,128)S(1)} %bitcast.41), channel_id=1, replica_groups=mesh['section'=2,'dp'=32,'tensor'=4] {'tensor'}, dimensions={0} | all-to-all | bytes 320 | tf_op jit(solution)/shard_map/all_to_all | solution.py:76
  249.7 0.5 broadcast.116
  250.2 0.7 reduce.3
  250.9 0.1 all_to_all.26
  251.0 18.5 %collective-permute-done.1 = s32[1,40]{1,0:T(1,128)S(1)} collective-permute-done((s32[1,40]{1,0:T(1,128)S(1)}, s32[1,40]{1,0:T(1,128)S(1)}, u32[]{:S(2)}, u32[]{:S(2)}) %collective-permute-start.1) | collective-permute-done | bytes 192 | tf_op jit(solution)/shard_map/ppermute | solution.py:22
  269.6 5.6 %fusion.2 = f32[128,40,128]{0,2,1:T(8,128)} fusion(bf16[128,40,128]{0,2,1:T(8,128)(2,1)} %bitcast.22, f32[40]{0:T(128)S(1)} %exponential_bitcast_fusion.1), kind=kOutput, calls=%fused_computation.5 | convolution fusion | flops 1008369664 | bytes 3932320 | tf_op jit(solution)/shard_map/aibj,jk->aibk/dot_general | solution.py:39
  275.1 3.2 %copy.21 = f32[1,128,5120]{2,1,0:T(8,128)} copy(f32[1,128,5120]{1,2,0:T(8,128)} %bitcast.37) | data formatting | bytes 5242880 | tf_op jit(solution)/shard_map/broadcast_in_dim;reshape | solution.py:105
  (16 shorter events, 0.1 us)
Async XLA Ops:
  6.5 127.8 %copy-start = (bf16[1,512,2048]{2,1,0:T(8,128)(2,1)S(1)}, bf16[1,512,2048]{2,1,0:T(8,128)(2,1)}, u32[]{:S(2)}) copy-start(bf16[1,512,2048]{2,1,0:T(8,128)(2,1)} %param.5) | copy-start | bytes 6291460
  6.5 127.8 %all-gather.3.cloned.1.call-start = ((), (), s32[]{:S(2)}) async-start(), calls=%async_computation.4 | async-start | bytes 21626880 | tf_op jit(solution)/shard_map/all_gather | solution.py:88
  7.3 202.9 %reduce-scatter.2.cloned.1.call-start = ((), (), s32[]{:S(2)}) async-start(), calls=%async_computation.3 | async-start | bytes 6553600 | tf_op jit(solution)/shard_map/reduce_scatter | solution.py:97
  7.3 141.1 %copy-start.1 = (bf16[1,512,1280]{2,1,0:T(8,128)(2,1)S(1)}, bf16[1,512,1280]{2,1,0:T(8,128)(2,1)}, u32[]{:S(2)}) copy-start(bf16[1,512,1280]{2,1,0:T(8,128)(2,1)} %param.7) | copy-start | bytes 3932164
  152.0 0.7 copy-start.3
  152.0 0.8 copy-start.2
  239.6 30.0 %collective-permute-start = (bf16[128,5120]{0,1:T(8,128)(2,1)S(1)}, bf16[128,5120]{0,1:T(8,128)(2,1)}, u32[]{:S(2)}, u32[]{:S(2)}) collective-permute-start(bf16[128,5120]{0,1:T(8,128)(2,1)S(1)} %bitcast.38), channel_id=1, source_target_pairs={{0,128},{128,0},{1,129},{129,1},{2,130},{130,2},{3,131},{131,3},{4... | collective-permute-start | bytes 3932168 | tf_op jit(solution)/shard_map/ppermute | solution.py:22
  251.0 18.6 %collective-permute-start.1 = (s32[1,40]{1,0:T(1,128)S(1)}, s32[1,40]{1,0:T(1,128)S(1)}, u32[]{:S(2)}, u32[]{:S(2)}) collective-permute-start(s32[1,40]{1,0:T(1,128)S(1)} %all_to_all.26), channel_id=1, source_target_pairs={{0,128},{128,0},{1,129},{129,1},{2,130},{130,2},{3,131},{131,3},{4... | collective-permute-start | bytes 488 | tf_op jit(solution)/shard_map/ppermute | solution.py:22
Sparse Core Ops, SparseCore 0:
  9.2 125.0 all-gather.2
  152.1 57.9 reduce-scatter.1
where the time goes:
time: 287 us; the launch traced here: 285 us
  waiting for transfers between devices  204 us (71%)
  blocking collectives  26.2 us (9%)
  matrix products  23.6 us (8%)
  between operations  13.5 us (5%)
  local copies, waits for them, and re-layouts  10.8 us (4%)
  other arithmetic  4.64 us (2%)
    all_gather x1, waiting for transfers between devices, shards(): lax.all_gather(weight[0], 'dp', axis=0, tiled=True)  127 us
    reduce_scatter x1, waiting for transfers between devices, shards(): lax.psum_scatter(partial_value.astype(jnp.bfloat16), 'tensor', scatter_di...  57.4 us
    all_to_all x1, blocking collectives, relayout(): lax.all_to_all(quant, 'tensor', split_axis=0, concat_axis=1, tiled=True)  19.4 us
    ppermute x2, waiting for transfers between devices, from_behind(): return lax.ppermute(value, axis, pairs)  18.5 us
    dot_general x1, matrix products, shards(): jnp.dot(left_rows, lax.all_gather(weight[0], 'dp', axis=0, tiled=True), p...  14 us
    dot_general x2, matrix products, rotate(): jnp.einsum('aibj,jk->aibk', tiles, table, precision=lax.Precision.HIGHEST)  9.55 us
    all_to_all x1, blocking collectives, relayout(): lax.all_to_all(exponent, 'tensor', split_axis=0, concat_axis=1, tiled=True)  6.83 us
  transfers between devices with their start and end apart: 4, of which 3 were waited for; matrix products, arithmetic and copies ran while one was open for 1% of the time, Pallas kernels for 0%

commit v1 on v0

v1 whole, which is shorter than its diff:
```python
import functools
import math

import jax
import jax.numpy as jnp
import numpy as np
from jax import lax
from jax.experimental import pallas as pl
from jax.experimental.pallas import tpu as pltpu
from jax.sharding import PartitionSpec as P

TILE = 128
N_T = 4
N_Z = 8
GROUP = 4
DP = N_Z * GROUP
WIDE = 640
DEPTH = 2048
FULL = 5120
ROOT = 1.0 / math.sqrt(TILE)
VMEM_LIMIT = 48 * 1024 * 1024
MIB = 1024 * 1024


def signs():
    index = np.arange(TILE)
    common = index[:, None] & index[None, :]
    parity = np.zeros((TILE, TILE), np.int64)
    for shift in range(7):
        parity += (common >> shift) & 1
    return jnp.asarray(1 - 2 * (parity & 1), jnp.bfloat16)


def call(body, out_shape, n_scalar, in_specs, out_specs, grid=(1,), scratch=(), cost=None):
    return pl.pallas_call(
        body,
        out_shape=out_shape,
        grid_spec=pltpu.PrefetchScalarGridSpec(
            num_scalar_prefetch=n_scalar,
            grid=grid,
            in_specs=in_specs,
            out_specs=out_specs,
            scratch_shapes=scratch,
        ),
        compiler_params=pltpu.CompilerParams(vmem_limit_bytes=VMEM_LIMIT),
        cost_estimate=cost,
    )


def whole(shape):
    return pl.BlockSpec(shape, lambda *_: (0,) * len(shape))


def bf16(*shape):
    return jax.ShapeDtypeStruct(shape, jnp.bfloat16)


def split_weight_body(sc, w_ref, *outs):
    x, c = sc[1], sc[2]
    for p, out in enumerate(outs):
        px, pc = x ^ (p >> 1), c ^ (p & 1)
        for u in range(2):
            start = pl.multiple_of((2 * pc + u) * 2 * WIDE + px * WIDE, 128)
            out[:, u * WIDE : (u + 1) * WIDE] = w_ref[:, pl.ds(start, WIDE)]


def split_weight(sc, weight):
    rows = weight.shape[0]
    return call(
        split_weight_body,
        [bf16(rows, 2 * WIDE)] * GROUP,
        1,
        [whole((rows, FULL))],
        [whole((rows, 2 * WIDE))] * GROUP,
        cost=pl.CostEstimate(flops=0, bytes_accessed=4 * rows * FULL, transcendentals=0),
    )(sc, weight)


def join_weight_body(sc, *refs):
    pieces, outs = refs[:GROUP], refs[GROUP:]
    own = sc[1] * 2 + sc[2]
    rows = pieces[0].shape[0]
    for p, piece in enumerate(pieces):
        start = pl.multiple_of((own ^ p) * rows, rows)
        for u, out in enumerate(outs):
            out[pl.ds(start, rows), :] = piece[:, u * WIDE : (u + 1) * WIDE]


def join_weight(sc, pieces):
    rows = pieces[0].shape[0]
    return call(
        join_weight_body,
        [bf16(GROUP * rows, WIDE)] * 2,
        1,
        [whole((rows, 2 * WIDE))] * GROUP,
        [whole((GROUP * rows, WIDE))] * 2,
        cost=pl.CostEstimate(flops=0, bytes_accessed=16 * rows * WIDE * 2, transcendentals=0),
    )(sc, *pieces)


def order_left_body(sc, left_ref, near_ref, far_ref, near_out, far_out):
    near_out[0, :, :DEPTH] = left_ref[...]
    far_out[0, :, :DEPTH] = left_ref[...]
    near_out[0, :, DEPTH:] = near_ref[...]
    far_out[0, :, DEPTH:] = far_ref[...]


def order_left(sc, left, base):
    def block(k, sc):
        want = (sc[0] + k) % N_T
        return sum(jnp.where(sc[4 + j] == want, j, 0) for j in range(N_T))

    return call(
        order_left_body,
        [bf16(N_T, TILE, DEPTH + WIDE)] * 2,
        1,
        [
            pl.BlockSpec((TILE, DEPTH), lambda k, sc: (block(k, sc), 0)),
            pl.BlockSpec((TILE, WIDE), lambda k, sc: (block(k, sc), sc[1])),
            pl.BlockSpec((TILE, WIDE), lambda k, sc: (block(k, sc), 1 - sc[1])),
        ],
        [pl.BlockSpec((1, TILE, DEPTH + WIDE), lambda k, sc: (k, 0, 0))] * 2,
        grid=(N_T,),
        cost=pl.CostEstimate(flops=0, bytes_accessed=10 * MIB, transcendentals=0),
    )(sc, left, base, base)


def product_body(chunk, n, sc, *refs):
    lefts, w_ref, outs = refs[:n], refs[n], refs[n + 1 :]
    k = pl.program_id(0)
    mine = jnp.where((sc[0] == 2 * sc[2] + chunk), 1.0, 0.0)
    for i in range(n):
        total = jnp.dot(lefts[i][0, :, :DEPTH], w_ref[...], preferred_element_type=jnp.float32)
        total = total + lefts[i][0, :, DEPTH:].astype(jnp.float32) * mine
        total = total.astype(jnp.bfloat16)
        for kk, out in enumerate(outs):

            @pl.when(k == kk)
            def _(out=out, i=i, total=total):
                out[i] = total


def product(sc, chunk, lefts, weight):
    n = len(lefts)
    return call(
        functools.partial(product_body, chunk, n),
        [bf16(n, TILE, WIDE)] * N_T,
        1,
        [pl.BlockSpec((1, TILE, DEPTH + WIDE), lambda k, sc: (k, 0, 0))] * n + [whole((DEPTH, WIDE))],
        [whole((n, TILE, WIDE))] * N_T,
        grid=(N_T,),
        cost=pl.CostEstimate(
            flops=2 * n * N_T * TILE * DEPTH * WIDE, bytes_accessed=(3 * n + 3) * MIB, transcendentals=0
        ),
    )(sc, *lefts, weight)


def turn_body(n, h_ref, *refs):
    parts, outs = refs[:N_T], refs[N_T:]
    for i, out in enumerate(outs):
        for j in range(WIDE // TILE):
            cols = slice(j * TILE, (j + 1) * TILE)
            total = jnp.dot(parts[0][i, :, cols], h_ref[...], preferred_element_type=jnp.float32)
            for part in parts[1:]:
                total += jnp.dot(part[i, :, cols], h_ref[...], preferred_element_type=jnp.float32)
            out[:, cols] = (total * ROOT).astype(jnp.bfloat16)


def turn(table, parts):
    n = parts[0].shape[0]
    return call(
        functools.partial(turn_body, n),
        [bf16(TILE, WIDE)] * n,
        0,
        [whole((TILE, TILE))] + [whole((n, TILE, WIDE))] * N_T,
        [whole((TILE, WIDE))] * n,
        cost=pl.CostEstimate(
            flops=8 * n * TILE * TILE * WIDE, bytes_accessed=n * MIB, transcendentals=0
        ),
    )(table, *parts)


def finish_body(sc, lim, h_ref, *refs):
    pieces, out = refs[:-1], refs[-1]
    x, c = sc[1], sc[2]
    for p in range(GROUP):
        for u in range(2):
            piece = pieces[2 * p + u]
            first = (2 * (c ^ (p & 1)) + u) * 10 + (x ^ (p >> 1)) * 5
            for j in range(WIDE // TILE):
                top = lim[first + j]
                value = piece[:, j * TILE : (j + 1) * TILE].astype(jnp.float32)
                value = jnp.clip(value, -top, top).astype(jnp.bfloat16)
                value = jnp.dot(value, h_ref[...], preferred_element_type=jnp.float32) * ROOT
                out[:, pl.ds(pl.multiple_of((first + j) * TILE, TILE), TILE)] = value


def finish(sc, lim, table, pieces):
    return call(
        finish_body,
        jax.ShapeDtypeStruct((TILE, FULL), jnp.float32),
        2,
        [whole((TILE, TILE))] + [whole((TILE, WIDE))] * len(pieces),
        whole((TILE, FULL)),
        cost=pl.CostEstimate(flops=2 * TILE * TILE * FULL, bytes_accessed=4 * MIB, transcendentals=0),
    )(sc, lim, table, *pieces)


def swap(value, offset):
    return lax.ppermute(value, "dp", [(i, i ^ offset) for i in range(DP)])


def cross(value, offset):
    pairs = [(s * DP + i, (1 - s) * DP + (i ^ offset)) for s in range(2) for i in range(DP)]
    return lax.ppermute(value, ("section", "dp"), pairs)


def along_y(value, steps):
    return lax.ppermute(value, "tensor", [(i, (i + steps) % N_T) for i in range(N_T)])


def gather_z(block):
    groups = [[z * GROUP + m for z in range(N_Z)] for m in range(GROUP)]
    return lax.all_gather(block, "dp", axis=0, tiled=True, axis_index_groups=groups)


def limits(expo, perm):
    here = lax.axis_index("tensor")
    other = 1 - lax.axis_index("section")
    top = 448.0 * jnp.exp2(expo.astype(jnp.float32))
    packed = jnp.concatenate([top, perm.astype(jnp.float32)[:, None]], axis=1)
    everyone = lax.all_gather(packed, ("section", "tensor"), axis=0).reshape(2, N_T, N_T, 11)
    theirs = lax.dynamic_index_in_dim(everyone, other, 0, keepdims=False)
    hit = theirs[:, :, 10] == here.astype(jnp.float32)
    return jnp.sum(jnp.where(hit[:, :, None], theirs[:, :, :10], 0.0), axis=1).reshape(-1)


def shards(left, weight, base, expo, perm):
    table = signs()
    dp = lax.axis_index("dp")
    sc = jnp.concatenate(
        [
            jnp.stack([lax.axis_index("tensor"), (dp // 2) % 2, dp % 2, dp // GROUP]).astype(jnp.int32),
            perm[0, 0],
        ]
    )
    pieces = split_weight(sc, weight[0])
    blocks = join_weight(sc, [pieces[0]] + [swap(pieces[p], p) for p in range(1, GROUP)])
    near, far = order_left(sc, left[0], base[0])
    far_x = swap(far, 2)
    near_c = swap(near, 1)
    far_xc = swap(far_x, 1)
    lim = limits(expo[0], perm[0, 0])
    arrived = {}
    for chunk in range(2):
        w = gather_z(blocks[chunk])
        for lefts, offsets in (((near, near_c), (0, 1)), ((far_x, far_xc), (2, 3))):
            parts = product(sc, chunk, lefts, w)
            parts = [parts[0]] + [along_y(parts[k], k) for k in range(1, N_T)]
            for offset, turned in zip(offsets, turn(table, parts)):
                arrived[offset, chunk] = cross(turned, offset)
    ordered = [arrived[p, u] for p in range(GROUP) for u in range(2)]
    return finish(sc, lim, table, ordered)[None]


def solution(mesh):
    in_specs = (
        P("section", "dp", "tensor"),
        P("section", ("tensor", "dp"), None),
        P("section", "dp", "tensor"),
        P("section", "dp", "tensor"),
        P("section", "dp", None),
    )
    out_specs = P("section", ("dp", "tensor"), None)
    return jax.shard_map(shards, mesh=mesh, in_specs=in_specs, out_specs=out_specs, check_vma=False)
```

time: 287 us -> 228 us (0.79)
  waiting for transfers between devices: 204 us -> 82 us
  starting transfers between devices: 2.75 us -> 47 us
  Pallas kernels: 0 us -> 41 us
  matrix products: 23.6 us -> 0 us
  local copies, waits for them, and re-layouts: 10.8 us -> 18.1 us
  other arithmetic: 4.64 us -> 0.18 us
    all_gather x1 -> x2, waiting for transfers between devices: 127 us -> 2.08 us  [gather_z(): lax.all_gather(block, 'dp', axis=0, tiled=True, axis_index_groups=groups)]
    ppermute x2 -> x26, waiting for transfers between devices: 18.5 us -> 79.9 us  [the longest x6 68.3 us: swap(): return lax.ppermute(value, 'dp', [(i, i ^ offset) for i in range(DP)])]
    reduce_scatter x1 -> x0, waiting for transfers between devices: 57.4 us -> none  [shards(): lax.psum_scatter(partial_value.astype(jnp.bfloat16), 'tensor', scatter_di...]
    ppermute x2 -> x26, starting transfers between devices: 2.71 us -> 47 us  [the longest x8 24.8 us: cross(): return lax.ppermute(value, ('section', 'dp'), pairs)]
    pallas_call x0 -> x12, Pallas kernels: none -> 41 us  [the longest x4 30.2 us: product(): call(functools.partial(product_body, chunk, n), [bf16(n, TILE, WIDE)] * N...]
    all_to_all x2 -> x0, blocking collectives: 26.2 us -> none  [the longest x1 19.4 us: relayout(): lax.all_to_all(quant, 'tensor', split_axis=0, concat_axis=1, tiled=True)]
    all_gather x0 -> x1, blocking collectives: none -> 25.7 us  [limits(): lax.all_gather(packed, ('section', 'tensor'), axis=0)]
    dot_general x3 -> x0, matrix products: 23.6 us -> none  [the longest x1 14 us: shards(): jnp.dot(left_rows, lax.all_gather(weight[0], 'dp', axis=0, tiled=True), p...]
  transfers between devices with their start and end apart: 4 -> 28, of which waited for: 3 -> 8; matrix products, arithmetic and copies ran while one was open for 1% -> 0% of each run, Pallas kernels for 0% -> 16%
where the time goes in v1:
time: 228 us
  waiting for transfers between devices  82 us (36%)
  starting transfers between devices  47 us (21%)
  Pallas kernels  41 us (18%)
  blocking collectives  25.7 us (11%)
  local copies, waits for them, and re-layouts  18.1 us (8%)
  between operations  13.5 us (6%)
    ppermute x6, waiting for transfers between devices, swap(): return lax.ppermute(value, 'dp', [(i, i ^ offset) for i in range(DP)])  68.3 us
    pallas_call x4, Pallas kernels, product(): call(functools.partial(product_body, chunk, n), [bf16(n, TILE, WIDE)] * N...  30.2 us
    all_gather x1, blocking collectives, limits(): lax.all_gather(packed, ('section', 'tensor'), axis=0)  25.7 us
    ppermute x8, starting transfers between devices, cross(): return lax.ppermute(value, ('section', 'dp'), pairs)  24.8 us
    unnamed x46, local copies, waits for them, and re-layouts  17 us
    ppermute x12, starting transfers between devices, along_y(): lax.ppermute(value, 'tensor', [(i, (i + steps) % N_T) for i in range(N_T)])  15.4 us
    ppermute x8, waiting for transfers between devices, cross(): return lax.ppermute(value, ('section', 'dp'), pairs)  11.5 us
    ppermute x6, starting transfers between devices, swap(): return lax.ppermute(value, 'dp', [(i, i ^ offset) for i in range(DP)])  6.83 us
  transfers between devices with their start and end apart: 28, of which 8 were waited for; matrix products, arithmetic and copies ran while one was open for 0% of the time, Pallas kernels for 16%

profile of v1, /device:TPU:1, one launch (start us, length us, event | category | flops | bytes accessed | tf_op | source)
XLA Modules:
  0.0 227.6 jit_solution(13360635961101592956)
XLA Ops:
  9.0 3.3 %collective-permute-start.1 = (bf16[64,1280]{1,0:T(8,128)(2,1)S(1)}, bf16[64,1280]{1,0:T(8,128)(2,1)S(1)}, u32[]{:S(2)}, u32[]{:S(2)}) collective-permute-start(bf16[64,1280]{1,0:T(8,128)(2,1)S(1)} %get-tuple-element.39), channel_id=1, source_target_pairs={{0,4},{4,0},{8,12},{12,8},{16,20},{20,16},{24,28},{28,24},{32,36},... | collective-permute-start | bytes 491528 | tf_op jit(solution)/shard_map/ppermute | solution.py:210
  14.0 4.0 %collective-permute-done.2.refs_2_ = bf16[64,1280]{1,0:T(8,128)(2,1)S(1)} collective-permute-done((bf16[64,1280]{1,0:T(8,128)(2,1)S(1)}, bf16[64,1280]{1,0:T(8,128)(2,1)S(1)}, u32[]{:S(2)}, u32[]{:S(2)}) %collective-permute-start.2) | collective-permute-done | bytes 163872 | tf_op jit(solution)/shard_map/ppermute | solution.py:210
  18.1 3.7 %collective-permute-done.3.refs_3_ = bf16[64,1280]{1,0:T(8,128)(2,1)S(1)} collective-permute-done((bf16[64,1280]{1,0:T(8,128)(2,1)S(1)}, bf16[64,1280]{1,0:T(8,128)(2,1)S(1)}, u32[]{:S(2)}, u32[]{:S(2)}) %collective-permute-start.3) | collective-permute-done | bytes 163872 | tf_op jit(solution)/shard_map/ppermute | solution.py:210
  26.2 2.9 %shard_map.64 = (bf16[4,128,2688]{2,1,0:T(8,128)(2,1)S(1)}, bf16[4,128,2688]{2,1,0:T(8,128)(2,1)}) custom-call(s32[8]{0:T(128)S(1)} %concatenate.6.sc, bf16[512,2048]{1,0:T(8,128)(2,1)S(1)} %bitcast.21, bf16[512,1280]{1,0:T(8,128)(2,1)S(1)} %bitcast.19, bf16[512,1280]{1,0:T(8,128)(2,1)S(1)} %bitcast.20), custom_call_target="tpu_custom_call" | custom-call | bytes 10485760 | tf_op jit(solution)/shard_map/pallas_call | solution.py:113
  29.9 60.6 %collective-permute-done.14.refs_0_ = bf16[4,128,2688]{2,1,0:T(8,128)(2,1)} collective-permute-done((bf16[4,128,2688]{2,1,0:T(8,128)(2,1)}, bf16[4,128,2688]{2,1,0:T(8,128)(2,1)}, u32[]{:S(2)}, u32[]{:S(2)}) %collective-permute-start.14) | collective-permute-done | bytes 2752544 | tf_op jit(solution)/shard_map/ppermute | solution.py:210
  93.3 7.6 %shard_map.67 = (bf16[2,128,640]{2,1,0:T(8,128)(2,1)S(1)}, bf16[2,128,640]{2,1,0:T(8,128)(2,1)}, bf16[2,128,640]{2,1,0:T(8,128)(2,1)S(1)}, bf16[2,128,640]{2,1,0:T(8,128)(2,1)S(1)}) custom-call(s32[8]{0:T(128)S(1)} %concatenate.6.sc, bf16[4,128,2688]{2,1,0:T(8,128)(2,1)} %copy-done.16, bf16[4,128,2688]{2,1,0:T(8,128)(2,1)} %collective-permute-done.refs_1_, ...), custom_call_target="tpu_custom_call" | custom-call | flops 2684354560 | bytes 9437184 | tf_op jit(solution)/shard_map/pallas_call | solution.py:145
  100.9 2.2 collective-permute-start.5
  104.1 2.1 all-gather.7.cloned.1.call-done.refs_2_
  108.0 7.1 %shard_map.69 = (bf16[2,128,640]{2,1,0:T(8,128)(2,1)S(1)}, bf16[2,128,640]{2,1,0:T(8,128)(2,1)S(1)}, bf16[2,128,640]{2,1,0:T(8,128)(2,1)S(1)}, bf16[2,128,640]{2,1,0:T(8,128)(2,1)S(1)}) custom-call(s32[8]{0:T(128)S(1)} %concatenate.6.sc, bf16[4,128,2688]{2,1,0:T(8,128)(2,1)} %copy-done.16, bf16[4,128,2688]{2,1,0:T(8,128)(2,1)} %collective-permute-done.refs_1_, ...), custom_call_target="tpu_custom_call" | custom-call | flops 2684354560 | bytes 9437184 | tf_op jit(solution)/shard_map/pallas_call | solution.py:145
  116.3 2.4 %collective-permute-start.9 = (bf16[2,128,640]{2,1,0:T(8,128)(2,1)S(1)}, bf16[2,128,640]{2,1,0:T(8,128)(2,1)S(1)}, u32[]{:S(2)}, u32[]{:S(2)}) collective-permute-start(bf16[2,128,640]{2,1,0:T(8,128)(2,1)S(1)} %get-tuple-element.51), channel_id=1, source_target_pairs={{0,2},{1,3},{2,0},{3,1},{4,6},{5,7},{6,4},{7,5},{8,10},{9,11},{10,... | collective-permute-start | bytes 983048 | tf_op jit(solution)/shard_map/ppermute | solution.py:219
  118.8 7.7 %shard_map.71 = (bf16[2,128,640]{2,1,0:T(8,128)(2,1)S(1)}, bf16[2,128,640]{2,1,0:T(8,128)(2,1)S(1)}, bf16[2,128,640]{2,1,0:T(8,128)(2,1)}, bf16[2,128,640]{2,1,0:T(8,128)(2,1)}) custom-call(s32[8]{0:T(128)S(1)} %concatenate.6.sc, bf16[4,128,2688]{2,1,0:T(8,128)(2,1)} %collective-permute-done.14.refs_0_, ...), custom_call_target="tpu_custom_call" | custom-call | flops 2684354560 | bytes 9437184 | tf_op jit(solution)/shard_map/pallas_call | solution.py:145
  128.7 7.8 %shard_map.73 = (bf16[2,128,640]{2,1,0:T(8,128)(2,1)S(1)}, bf16[2,128,640]{2,1,0:T(8,128)(2,1)}, bf16[2,128,640]{2,1,0:T(8,128)(2,1)}, bf16[2,128,640]{2,1,0:T(8,128)(2,1)}) custom-call(s32[8]{0:T(128)S(1)} %concatenate.6.sc, bf16[4,128,2688]{2,1,0:T(8,128)(2,1)} %collective-permute-done.14.refs_0_, bf16[4,128,2688]{2,1,0:T(8,128)(2,1)} %collective-permute-done.15.refs_1_, ...), custom_call_target="tpu_custom_call" | custom-call | flops 2684354560 | bytes 9437184 | tf_op jit(solution)/shard_map/pallas_call | solution.py:145
  142.5 1.8 collective-permute-start.21
  144.3 2.1 collective-permute-start.22
  154.0 2.8 %collective-permute-start.7 = (bf16[128,640]{1,0:T(8,128)(2,1)}, bf16[128,640]{1,0:T(8,128)(2,1)S(1)}, u32[]{:S(2)}, u32[]{:S(2)}) collective-permute-start(bf16[128,640]{1,0:T(8,128)(2,1)} %get-tuple-element.47), channel_id=1, source_target_pairs={{0,128},{4,132},{8,136},{12,140},{16,144},{20,148},{24,152},{28,15... | collective-permute-start | bytes 491528 | tf_op jit(solution)/shard_map/ppermute | solution.py:215
  158.1 8.3 %collective-permute-start.12 = (bf16[128,640]{1,0:T(8,128)(2,1)}, bf16[128,640]{1,0:T(8,128)(2,1)S(1)}, u32[]{:S(2)}, u32[]{:S(2)}) collective-permute-start(bf16[128,640]{1,0:T(8,128)(2,1)} %get-tuple-element.54), channel_id=1, source_target_pairs={{0,132},{4,128},{8,140},{12,136},{16,148},{20,144},{24,156},{28,15... | collective-permute-start | bytes 491528 | tf_op jit(solution)/shard_map/ppermute | solution.py:215
  166.4 25.7 %all-gather.1 = f32[8,4,11]{2,1,0:T(4,128)S(1)} all-gather(f32[1,4,11]{2,1,0:T(4,128)S(1)} %maximum_bitcast_fusion), channel_id=2, replica_groups=mesh['section'=2,'dp'=32,'tensor'=4] {'section','tensor'}, dimensions={0}, use_global_device_ids=true | all-gather | bytes 1584 | tf_op jit(solution)/shard_map/all_gather | solution.py:232
  193.4 6.7 %collective-permute-start.13 = (bf16[128,640]{1,0:T(8,128)(2,1)S(1)}, bf16[128,640]{1,0:T(8,128)(2,1)S(1)}, u32[]{:S(2)}, u32[]{:S(2)}) collective-permute-start(bf16[128,640]{1,0:T(8,128)(2,1)S(1)} %get-tuple-element.55), channel_id=1, source_target_pairs={{0,132},{4,128},{8,140},{12,136},{16,148},{20,144},{24,156},{28,15... | collective-permute-start | bytes 491528 | tf_op jit(solution)/shard_map/ppermute | solution.py:215
  201.5 1.9 collective-permute-start.23
  203.8 2.6 %collective-permute-start.25 = (bf16[128,640]{1,0:T(8,128)(2,1)S(1)}, bf16[128,640]{1,0:T(8,128)(2,1)S(1)}, u32[]{:S(2)}, u32[]{:S(2)}) collective-permute-start(bf16[128,640]{1,0:T(8,128)(2,1)S(1)} %get-tuple-element.68), channel_id=1, source_target_pairs={{0,140},{4,136},{8,132},{12,128},{16,156},{20,152},{24,148},{28,14... | collective-permute-start | bytes 491528 | tf_op jit(solution)/shard_map/ppermute | solution.py:215
  207.8 3.3 %collective-permute-done.23.refs_5_ = bf16[128,640]{1,0:T(8,128)(2,1)S(1)} collective-permute-done((bf16[128,640]{1,0:T(8,128)(2,1)S(1)}, bf16[128,640]{1,0:T(8,128)(2,1)S(1)}, u32[]{:S(2)}, u32[]{:S(2)}) %collective-permute-start.23) | collective-permute-done | bytes 163872 | tf_op jit(solution)/shard_map/ppermute | solution.py:215
  211.1 3.5 %collective-permute-done.24.refs_6_ = bf16[128,640]{1,0:T(8,128)(2,1)S(1)} collective-permute-done((bf16[128,640]{1,0:T(8,128)(2,1)}, bf16[128,640]{1,0:T(8,128)(2,1)S(1)}, u32[]{:S(2)}, u32[]{:S(2)}) %collective-permute-start.24) | collective-permute-done | bytes 163872 | tf_op jit(solution)/shard_map/ppermute | solution.py:215
  214.6 3.5 %collective-permute-done.25.refs_7_ = bf16[128,640]{1,0:T(8,128)(2,1)S(1)} collective-permute-done((bf16[128,640]{1,0:T(8,128)(2,1)S(1)}, bf16[128,640]{1,0:T(8,128)(2,1)S(1)}, u32[]{:S(2)}, u32[]{:S(2)}) %collective-permute-start.25) | collective-permute-done | bytes 163872 | tf_op jit(solution)/shard_map/ppermute | solution.py:215
  218.2 2.6 %shard_map.75 = f32[128,5120]{1,0:T(8,128)} custom-call(s32[8]{0:T(128)S(1)} %concatenate.6.sc, f32[40]{0:T(128)S(1)} %reshape.24.lim, bf16[128,128]{1,0:T(8,128)(2,1)S(1)} %copy-done.2, bf16[128,640]{1,0:T(8,128)(2,1)S(1)} %collective-permute-done.7.refs_0_, bf16[128,640]{1,0:T(8,128)(2,1)S(1)} %collective-permute-done.11.refs_1_, ...), custom_call_target="tpu_custom_call" | custom-call | flops 167772160 | bytes 4194304 | tf_op jit(solution)/shard_map/pallas_call | solution.py:199
  (104 shorter events, 37.8 us)
Async XLA Ops:
  6.5 85.0 %all-gather.5.cloned.1.call-start = ((), (), s32[]{:S(2)}) async-start(), calls=%async_computation | async-start | bytes 2949120 | tf_op jit(solution)/shard_map/all_gather | solution.py:224
  23.2 83.0 %all-gather.7.cloned.1.call-start = ((), (), s32[]{:S(2)}) async-start(), calls=%async_computation.1 | async-start | bytes 2949120 | tf_op jit(solution)/shard_map/all_gather | solution.py:224
  29.1 61.4 %collective-permute-start.14 = (bf16[4,128,2688]{2,1,0:T(8,128)(2,1)}, bf16[4,128,2688]{2,1,0:T(8,128)(2,1)}, u32[]{:S(2)}, u32[]{:S(2)}) collective-permute-start(bf16[4,128,2688]{2,1,0:T(8,128)(2,1)} %get-tuple-element.56), channel_id=1, source_target_pairs={{0,8},{4,12},{8,0},{12,4},{16,24},{20,28},{24,16},{28,20},{32,40},... | collective-permute-start | bytes 8257544 | tf_op jit(solution)/shard_map/ppermute | solution.py:210
  29.1 62.4 %collective-permute-start = (bf16[4,128,2688]{2,1,0:T(8,128)(2,1)S(1)}, bf16[4,128,2688]{2,1,0:T(8,128)(2,1)}, u32[]{:S(2)}, u32[]{:S(2)}) collective-permute-start(bf16[4,128,2688]{2,1,0:T(8,128)(2,1)S(1)} %get-tuple-element.37.refs_0_), channel_id=1, source_target_pairs={{0,4},{4,0},{8,12},{12,8},{16,20},{20,16},{24,28},{28,24},{32,36},... | collective-permute-start | bytes 8257544 | tf_op jit(solution)/shard_map/ppermute | solution.py:210
  90.5 25.8 %collective-permute-start.15 = (bf16[4,128,2688]{2,1,0:T(8,128)(2,1)}, bf16[4,128,2688]{2,1,0:T(8,128)(2,1)}, u32[]{:S(2)}, u32[]{:S(2)}) collective-permute-start(bf16[4,128,2688]{2,1,0:T(8,128)(2,1)} %collective-permute-done.14.refs_0_), channel_id=1, source_target_pairs={{0,4},{4,0},{8,12},{12,8},{16,20},{20,16},{24,28},{28,24},{32,36},... | collective-permute-start | bytes 8257544 | tf_op jit(solution)/shard_map/ppermute | solution.py:210
  100.9 25.6 %collective-permute-start.4 = (bf16[2,128,640]{2,1,0:T(8,128)(2,1)}, bf16[2,128,640]{2,1,0:T(8,128)(2,1)S(1)}, u32[]{:S(2)}, u32[]{:S(2)}) collective-permute-start(bf16[2,128,640]{2,1,0:T(8,128)(2,1)} %get-tuple-element.44), channel_id=1, source_target_pairs={{0,1},{1,2},{2,3},{3,0},{4,5},{5,6},{6,7},{7,4},{8,9},{9,10},{10,1... | collective-permute-start | bytes 983048 | tf_op jit(solution)/shard_map/ppermute | solution.py:219
  100.9 26.9 %collective-permute-start.5 = (bf16[2,128,640]{2,1,0:T(8,128)(2,1)S(1)}, bf16[2,128,640]{2,1,0:T(8,128)(2,1)S(1)}, u32[]{:S(2)}, u32[]{:S(2)}) collective-permute-start(bf16[2,128,640]{2,1,0:T(8,128)(2,1)S(1)} %get-tuple-element.45), channel_id=1, source_target_pairs={{0,2},{1,3},{2,0},{3,1},{4,6},{5,7},{6,4},{7,5},{8,10},{9,11},{10,... | collective-permute-start | bytes 983048 | tf_op jit(solution)/shard_map/ppermute | solution.py:219
  103.1 33.5 %collective-permute-start.6 = (bf16[2,128,640]{2,1,0:T(8,128)(2,1)S(1)}, bf16[2,128,640]{2,1,0:T(8,128)(2,1)S(1)}, u32[]{:S(2)}, u32[]{:S(2)}) collective-permute-start(bf16[2,128,640]{2,1,0:T(8,128)(2,1)S(1)} %get-tuple-element.46), channel_id=1, source_target_pairs={{0,3},{1,0},{2,1},{3,2},{4,7},{5,4},{6,5},{7,6},{8,11},{9,8},{10,9... | collective-permute-start | bytes 983048 | tf_op jit(solution)/shard_map/ppermute | solution.py:219
  115.0 23.2 %collective-permute-start.8 = (bf16[2,128,640]{2,1,0:T(8,128)(2,1)S(1)}, bf16[2,128,640]{2,1,0:T(8,128)(2,1)S(1)}, u32[]{:S(2)}, u32[]{:S(2)}) collective-permute-start(bf16[2,128,640]{2,1,0:T(8,128)(2,1)S(1)} %get-tuple-element.50), channel_id=1, source_target_pairs={{0,1},{1,2},{2,3},{3,0},{4,5},{5,6},{6,7},{7,4},{8,9},{9,10},{10,1... | collective-permute-start | bytes 983048 | tf_op jit(solution)/shard_map/ppermute | solution.py:219
  116.3 24.2 %collective-permute-start.9 = (bf16[2,128,640]{2,1,0:T(8,128)(2,1)S(1)}, bf16[2,128,640]{2,1,0:T(8,128)(2,1)S(1)}, u32[]{:S(2)}, u32[]{:S(2)}) collective-permute-start(bf16[2,128,640]{2,1,0:T(8,128)(2,1)S(1)} %get-tuple-element.51), channel_id=1, source_target_pairs={{0,2},{1,3},{2,0},{3,1},{4,6},{5,7},{6,4},{7,5},{8,10},{9,11},{10,... | collective-permute-start | bytes 983048 | tf_op jit(solution)/shard_map/ppermute | solution.py:219
  126.5 15.3 %collective-permute-start.10 = (bf16[2,128,640]{2,1,0:T(8,128)(2,1)S(1)}, bf16[2,128,640]{2,1,0:T(8,128)(2,1)S(1)}, u32[]{:S(2)}, u32[]{:S(2)}) collective-permute-start(bf16[2,128,640]{2,1,0:T(8,128)(2,1)S(1)} %get-tuple-element.52), channel_id=1, source_target_pairs={{0,3},{1,0},{2,1},{3,2},{4,7},{5,4},{6,5},{7,6},{8,11},{9,8},{10,9... | collective-permute-start | bytes 983048 | tf_op jit(solution)/shard_map/ppermute | solution.py:219
  128.5 15.8 %collective-permute-start.16 = (bf16[2,128,640]{2,1,0:T(8,128)(2,1)S(1)}, bf16[2,128,640]{2,1,0:T(8,128)(2,1)S(1)}, u32[]{:S(2)}, u32[]{:S(2)}) collective-permute-start(bf16[2,128,640]{2,1,0:T(8,128)(2,1)S(1)} %get-tuple-element.58), channel_id=1, source_target_pairs={{0,1},{1,2},{2,3},{3,0},{4,5},{5,6},{6,7},{7,4},{8,9},{9,10},{10,1... | collective-permute-start | bytes 983048 | tf_op jit(solution)/shard_map/ppermute | solution.py:219
  137.3 16.7 %collective-permute-start.17 = (bf16[2,128,640]{2,1,0:T(8,128)(2,1)}, bf16[2,128,640]{2,1,0:T(8,128)(2,1)S(1)}, u32[]{:S(2)}, u32[]{:S(2)}) collective-permute-start(bf16[2,128,640]{2,1,0:T(8,128)(2,1)} %get-tuple-element.59), channel_id=1, source_target_pairs={{0,2},{1,3},{2,0},{3,1},{4,6},{5,7},{6,4},{7,5},{8,10},{9,11},{10,... | collective-permute-start | bytes 983048 | tf_op jit(solution)/shard_map/ppermute | solution.py:219
  139.0 17.8 %collective-permute-start.18 = (bf16[2,128,640]{2,1,0:T(8,128)(2,1)}, bf16[2,128,640]{2,1,0:T(8,128)(2,1)S(1)}, u32[]{:S(2)}, u32[]{:S(2)}) collective-permute-start(bf16[2,128,640]{2,1,0:T(8,128)(2,1)} %get-tuple-element.60), channel_id=1, source_target_pairs={{0,3},{1,0},{2,1},{3,2},{4,7},{5,4},{6,5},{7,6},{8,11},{9,8},{10,9... | collective-permute-start | bytes 983048 | tf_op jit(solution)/shard_map/ppermute | solution.py:219
  141.2 16.9 %collective-permute-start.20 = (bf16[2,128,640]{2,1,0:T(8,128)(2,1)}, bf16[2,128,640]{2,1,0:T(8,128)(2,1)S(1)}, u32[]{:S(2)}, u32[]{:S(2)}) collective-permute-start(bf16[2,128,640]{2,1,0:T(8,128)(2,1)} %get-tuple-element.63), channel_id=1, source_target_pairs={{0,1},{1,2},{2,3},{3,0},{4,5},{5,6},{6,7},{7,4},{8,9},{9,10},{10,1... | collective-permute-start | bytes 983048 | tf_op jit(solution)/shard_map/ppermute | solution.py:219
  142.5 50.9 %collective-permute-start.21 = (bf16[2,128,640]{2,1,0:T(8,128)(2,1)}, bf16[2,128,640]{2,1,0:T(8,128)(2,1)S(1)}, u32[]{:S(2)}, u32[]{:S(2)}) collective-permute-start(bf16[2,128,640]{2,1,0:T(8,128)(2,1)} %get-tuple-element.64), channel_id=1, source_target_pairs={{0,2},{1,3},{2,0},{3,1},{4,6},{5,7},{6,4},{7,5},{8,10},{9,11},{10,... | collective-permute-start | bytes 983048 | tf_op jit(solution)/shard_map/ppermute | solution.py:219
  144.3 55.8 %collective-permute-start.22 = (bf16[2,128,640]{2,1,0:T(8,128)(2,1)}, bf16[2,128,640]{2,1,0:T(8,128)(2,1)S(1)}, u32[]{:S(2)}, u32[]{:S(2)}) collective-permute-start(bf16[2,128,640]{2,1,0:T(8,128)(2,1)} %get-tuple-element.65), channel_id=1, source_target_pairs={{0,3},{1,0},{2,1},{3,2},{4,7},{5,4},{6,5},{7,6},{8,11},{9,8},{10,9... | collective-permute-start | bytes 983048 | tf_op jit(solution)/shard_map/ppermute | solution.py:219
  154.0 47.5 %collective-permute-start.7 = (bf16[128,640]{1,0:T(8,128)(2,1)}, bf16[128,640]{1,0:T(8,128)(2,1)S(1)}, u32[]{:S(2)}, u32[]{:S(2)}) collective-permute-start(bf16[128,640]{1,0:T(8,128)(2,1)} %get-tuple-element.47), channel_id=1, source_target_pairs={{0,128},{4,132},{8,136},{12,140},{16,144},{20,148},{24,152},{28,15... | collective-permute-start | bytes 491528 | tf_op jit(solution)/shard_map/ppermute | solution.py:215
  156.8 46.7 %collective-permute-start.11 = (bf16[128,640]{1,0:T(8,128)(2,1)S(1)}, bf16[128,640]{1,0:T(8,128)(2,1)S(1)}, u32[]{:S(2)}, u32[]{:S(2)}) collective-permute-start(bf16[128,640]{1,0:T(8,128)(2,1)S(1)} %get-tuple-element.53), channel_id=1, source_target_pairs={{0,128},{4,132},{8,136},{12,140},{16,144},{20,148},{24,152},{28,15... | collective-permute-start | bytes 491528 | tf_op jit(solution)/shard_map/ppermute | solution.py:215
  158.1 45.7 %collective-permute-start.12 = (bf16[128,640]{1,0:T(8,128)(2,1)}, bf16[128,640]{1,0:T(8,128)(2,1)S(1)}, u32[]{:S(2)}, u32[]{:S(2)}) collective-permute-start(bf16[128,640]{1,0:T(8,128)(2,1)} %get-tuple-element.54), channel_id=1, source_target_pairs={{0,132},{4,128},{8,140},{12,136},{16,148},{20,144},{24,156},{28,15... | collective-permute-start | bytes 491528 | tf_op jit(solution)/shard_map/ppermute | solution.py:215
  193.4 13.3 %collective-permute-start.13 = (bf16[128,640]{1,0:T(8,128)(2,1)S(1)}, bf16[128,640]{1,0:T(8,128)(2,1)S(1)}, u32[]{:S(2)}, u32[]{:S(2)}) collective-permute-start(bf16[128,640]{1,0:T(8,128)(2,1)S(1)} %get-tuple-element.55), channel_id=1, source_target_pairs={{0,132},{4,128},{8,140},{12,136},{16,148},{20,144},{24,156},{28,15... | collective-permute-start | bytes 491528 | tf_op jit(solution)/shard_map/ppermute | solution.py:215
  201.5 9.6 %collective-permute-start.23 = (bf16[128,640]{1,0:T(8,128)(2,1)S(1)}, bf16[128,640]{1,0:T(8,128)(2,1)S(1)}, u32[]{:S(2)}, u32[]{:S(2)}) collective-permute-start(bf16[128,640]{1,0:T(8,128)(2,1)S(1)} %get-tuple-element.66), channel_id=1, source_target_pairs={{0,136},{4,140},{8,128},{12,132},{16,152},{20,156},{24,144},{28,14... | collective-permute-start | bytes 491528 | tf_op jit(solution)/shard_map/ppermute | solution.py:215
  203.4 11.2 %collective-permute-start.24 = (bf16[128,640]{1,0:T(8,128)(2,1)}, bf16[128,640]{1,0:T(8,128)(2,1)S(1)}, u32[]{:S(2)}, u32[]{:S(2)}) collective-permute-start(bf16[128,640]{1,0:T(8,128)(2,1)} %get-tuple-element.67), channel_id=1, source_target_pairs={{0,140},{4,136},{8,132},{12,128},{16,156},{20,152},{24,148},{28,14... | collective-permute-start | bytes 491528 | tf_op jit(solution)/shard_map/ppermute | solution.py:215
  203.8 14.4 %collective-permute-start.25 = (bf16[128,640]{1,0:T(8,128)(2,1)S(1)}, bf16[128,640]{1,0:T(8,128)(2,1)S(1)}, u32[]{:S(2)}, u32[]{:S(2)}) collective-permute-start(bf16[128,640]{1,0:T(8,128)(2,1)S(1)} %get-tuple-element.68), channel_id=1, source_target_pairs={{0,140},{4,136},{8,132},{12,128},{16,156},{20,152},{24,148},{28,14... | collective-permute-start | bytes 491528 | tf_op jit(solution)/shard_map/ppermute | solution.py:215
  (27 other events, 191.3 us)
Sparse Core Ops, SparseCore 0:
  23.3 40.1 all-gather.4
  65.3 40.9 all-gather.6
